TPU v7x, 32 devices: a whole 2x2x4 slice. The times are simulated.
32 devices in a mesh: sta: 8 (over z, y), win: 4 (over x, core).
Axes of the slice: x: 2, y: 2, z: 4, core: 2. Of those that a mesh axis runs over, the one named last changes fastest.
Arguments:
- spectra: bfloat16 [64, 56, 4096], P('win', 'sta'), may hold values from -6 to 6
- pair_bins: int32 [56, 3, 7], P('sta'), may hold values from 0 to 15
- owner_count: int32 [8], replicated, may hold values from 1 to 4, 16 in all
- bin_order: int32 [16], replicated, may hold values from 0 to 15, each once
Outputs:
- owned_stacks: float32 [32, 4096], P('sta', 'win')
Inputs may be any that keep to these rules, and one draw needn't show every extreme that they name: Owner o holds owner_count[o] bins; the counts sum to 16 and the largest is exactly 4. `bin_order`: every bin appears exactly once.
All inputs are finite; a program needn't handle non-finite values.
Results may differ from a plain program's by a relative error of at most 0.0011.
Values may be sent and summed in bfloat16 or wider, within the bound.
A program may use at most 128 MiB of HBM per device.

v0:
```python
import functools
import jax
import jax.numpy as jnp
from jax import lax
from jax.experimental import pallas as pl
from jax.experimental.pallas import tpu as pltpu
from jax.sharding import PartitionSpec as P

CAP = 4
LANES = 128
ROWS = 8
MESH = pl.DeviceIdType.MESH


def passed_along(value, axis, steps):
    count = lax.axis_size(axis)
    pairs = [(source, (source + steps) % count) for source in range(count)]
    return lax.ppermute(value, axis, pairs)


def cross_pairs(own, other):
    width = own.shape[-1] // 2
    own_re, own_im = (own[..., :width], own[..., width:])
    other_re, other_im = (other[..., :width], other[..., width:])
    form = "wsf,wtf->stf"
    real = jnp.einsum(form, own_re, other_re, preferred_element_type=jnp.float32) + jnp.einsum(
        form, own_im, other_im, preferred_element_type=jnp.float32
    )
    imag = jnp.einsum(form, own_im, other_re, preferred_element_type=jnp.float32) - jnp.einsum(
        form, own_re, other_im, preferred_element_type=jnp.float32
    )
    joined = jnp.concatenate([real, imag], axis=-1).astype(jnp.bfloat16)
    return joined.reshape(-1, joined.shape[-1])


def by_blocks(spectra, pair_bins, owner_count, bin_order):
    rounds = pair_bins.shape[1]
    blocks = [spectra]
    for offset in range(1, rounds):
        blocks.append(passed_along(spectra, "sta", offset))
    crossed = jnp.concatenate([cross_pairs(spectra, other) for other in blocks], axis=0)
    labels = jnp.transpose(pair_bins, (1, 0, 2)).reshape(-1)
    bin_total = bin_order.shape[0]
    starts = jnp.cumsum(owner_count) - owner_count
    ranks = jnp.arange(CAP, dtype=jnp.int32)
    positions = jnp.clip(starts[:, None] + ranks[None, :], 0, bin_total - 1)
    valid = ranks[None, :] < owner_count[:, None]
    chosen = jnp.take(bin_order, positions)
    slot_bin = jnp.where(valid, chosen, -1).reshape(-1)
    window_total = spectra.shape[0] * lax.axis_size("win")
    matches = (slot_bin[:, None] == labels[None, :]).astype(jnp.bfloat16)
    partial_sums = jnp.dot(matches, crossed, preferred_element_type=jnp.float32)
    spread = lax.psum_scatter(partial_sums, "win", scatter_dimension=1, tiled=True)
    stacks = lax.psum_scatter(spread, "sta", scatter_dimension=0, tiled=True)
    return stacks * jnp.float32(1.0 / window_total)


def kernel(
    sizes, spec_ref, bins_ref, count_ref, order_ref, out_ref,
    recv, wide, lab, slots, crossed, total, outbox, inbox,
    send_sem, recv_sem, own_sem, lab_send, lab_recv, box_send, box_recv,
):
    n_sta, n_win, chunks, windows, stations, rounds, width = sizes
    share = width // n_sta
    out_cols = out_ref.shape[1]
    per_out = out_cols // share
    halves = width // out_cols
    me = lax.axis_index("sta")
    g = lax.axis_index("win")

    barrier = pltpu.get_barrier_semaphore()
    for t in range(1, n_sta * n_win):
        flat = lax.rem(me * n_win + g + t, n_sta * n_win)
        pl.semaphore_signal(
            barrier, inc=1, device_id=(flat // n_win, lax.rem(flat, n_win)), device_id_type=MESH
        )
    pl.semaphore_wait(barrier, n_sta * n_win - 1)

    def share_of(dest, c, part):
        col = pl.multiple_of(part * width + dest * share + c * LANES, LANES)
        return spec_ref.at[:, :, pl.ds(col, LANES)]

    def spectra_copy(c, k, part):
        dest = lax.rem(me + k, n_sta)
        return pltpu.make_async_remote_copy(
            src_ref=share_of(dest, c, part),
            dst_ref=recv.at[c, me, part],
            send_sem=send_sem.at[c, k, part],
            recv_sem=recv_sem.at[c, me, part],
            device_id=(dest, g),
            device_id_type=MESH,
        )

    def own_copy(c, part):
        return pltpu.make_async_copy(share_of(me, c, part), recv.at[c, me, part], own_sem.at[c, part])

    for c in range(chunks):
        for k in range(1, n_sta):
            for part in range(2):
                spectra_copy(c, k, part).start()
        for part in range(2):
            own_copy(c, part).start()

    lane = lax.broadcasted_iota(jnp.int32, (1, lab.shape[2]), 1)
    row = jnp.full((1, lab.shape[2]), -2, jnp.int32)
    for r in range(rounds):
        for j in range(stations):
            for i in range(stations):
                row = jnp.where(lane == (r * ROWS + j) * ROWS + i, bins_ref[r, i, j], row)
    lab[pl.ds(me, 1)] = row[None]

    def label_copy(k):
        return pltpu.make_async_remote_copy(
            src_ref=lab.at[me],
            dst_ref=lab.at[me],
            send_sem=lab_send.at[k],
            recv_sem=lab_recv.at[me],
            device_id=(lax.rem(me + k, n_sta), g),
            device_id_type=MESH,
        )

    for k in range(1, n_sta):
        label_copy(k).start()

    sub = lax.broadcasted_iota(jnp.int32, (n_sta * CAP, LANES), 0)
    slot = jnp.full((n_sta * CAP, LANES), -1, jnp.int32)
    start = jnp.int32(0)
    for o in range(n_sta):
        held = count_ref[o]
        for k in range(CAP):
            chosen = order_ref[jnp.clip(start + k, 0, order_ref.shape[0] - 1)]
            slot = jnp.where(sub == o * CAP + k, jnp.where(k < held, chosen, -1), slot)
        start = start + held
    slots[...] = slot

    wide[...] = jnp.zeros_like(wide)
    crossed[...] = jnp.zeros_like(crossed)
    for k in range(1, n_sta):
        src = lax.rem(me - k + n_sta, n_sta)
        pltpu.make_async_remote_copy(
            src_ref=lab.at[src], dst_ref=lab.at[src], send_sem=lab_send.at[k],
            recv_sem=lab_recv.at[src], device_id=(src, g), device_id_type=MESH,
        ).wait_recv()

    def widen(c, p):
        for part in range(2):
            for j in range(stations):
                wide[p, part, pl.ds(j, windows, stride=ROWS), :] = recv[c, p, part, j].astype(jnp.float32)

    def arrive(c, k):
        src = lax.rem(me - k + n_sta, n_sta)
        for part in range(2):
            pltpu.make_async_remote_copy(
                src_ref=recv.at[c, src, part], dst_ref=recv.at[c, src, part],
                send_sem=send_sem.at[c, k, part], recv_sem=recv_sem.at[c, src, part],
                device_id=(src, g), device_id_type=MESH,
            ).wait_recv()
        widen(c, src)

    def step(p):
        blocks = [lax.rem(p + r, n_sta) for r in range(rounds)]
        re = [[None] * stations for _ in range(rounds)]
        im = [[None] * stations for _ in range(rounds)]
        for w in range(windows):
            at = pl.ds(w * ROWS, ROWS)
            mine = [(wide[b, 0, at, :], wide[b, 1, at, :]) for b in blocks]
            for j in range(stations):
                a = jnp.broadcast_to(wide[p, 0, pl.ds(w * ROWS + j, 1), :], (ROWS, LANES))
                b = jnp.broadcast_to(wide[p, 1, pl.ds(w * ROWS + j, 1), :], (ROWS, LANES))
                for r in range(rounds):
                    x, y = mine[r]
                    if w == 0:
                        re[r][j] = x * a + y * b
                        im[r][j] = y * a - x * b
                    else:
                        re[r][j] = re[r][j] + x * a + y * b
                        im[r][j] = im[r][j] + y * a - x * b
        blank = jnp.zeros((ROWS, LANES), jnp.float32)
        for r in range(rounds):
            at = pl.ds(r * ROWS * ROWS, ROWS * ROWS)
            pad = [blank] * (ROWS - stations)
            crossed[at, 0:LANES] = jnp.concatenate(re[r] + pad, axis=0).astype(jnp.bfloat16)
            crossed[at, LANES:] = jnp.concatenate(im[r] + pad, axis=0).astype(jnp.bfloat16)
        lanes = lax.broadcasted_iota(jnp.int32, (1, lab.shape[2]), 1)
        names = jnp.full((1, lab.shape[2]), -2, jnp.int32)
        for r in range(rounds):
            names = jnp.where(lanes // (ROWS * ROWS) == r, lab[blocks[r]], names)
        match = jnp.concatenate(
            [slots[...] == names[:, at:at + LANES] for at in range(0, lab.shape[2], LANES)], axis=1
        )
        match = jnp.where(match, 1.0, 0.0).astype(jnp.bfloat16)
        return jnp.dot(match, crossed[...], preferred_element_type=jnp.float32)

    def box_copies(c, o, part):
        q = part * halves + me // per_out
        t = lax.rem(me, per_out)
        col = pl.multiple_of(t * share + c * LANES, LANES)
        src = outbox.at[c, part, o]
        dst = inbox.at[g, :, pl.ds(col, LANES)]

        def far():
            return pltpu.make_async_remote_copy(
                src_ref=src, dst_ref=dst, send_sem=box_send.at[c, part, o],
                recv_sem=box_recv.at[c, t, g], device_id=(o, q), device_id_type=MESH,
            )

        def near():
            return pltpu.make_async_copy(src, dst, box_recv.at[c, t, g])

        return far, near, jnp.logical_and(o == me, q == g)

    def one_chunk(c, carry):
        for part in range(2):
            own_copy(c, part).wait()
        widen(c, me)
        arrive(c, 1)
        total[...] = jnp.zeros_like(total)

        def one_step(k, carry):
            @pl.when(k < n_sta)
            def _():
                arrive(c, k)

            total[...] += step(lax.rem(me - k + 2 * n_sta, n_sta))
            return carry

        lax.fori_loop(rounds - 1, n_sta + rounds - 1, one_step, 0)
        for part in range(2):
            for o in range(n_sta):
                outbox[c, part, o] = total[o * CAP:(o + 1) * CAP, part * LANES:(part + 1) * LANES]
        for part in range(2):
            for o in range(n_sta):
                far, near, is_me = box_copies(c, o, part)
                pl.when(is_me)(lambda near=near: near().start())
                pl.when(jnp.logical_not(is_me))(lambda far=far: far().start())
        return carry

    lax.fori_loop(0, chunks, one_chunk, 0)

    for c in range(chunks):
        for t in range(per_out):
            for s in range(n_win):
                dst = inbox.at[s, :, pl.ds(t * share + c * LANES, LANES)]
                pltpu.make_async_copy(dst, dst, box_recv.at[c, t, s]).wait()
    out_ref[...] = functools.reduce(jnp.add, [inbox[s] for s in range(n_win)])

    for c in range(chunks):
        for k in range(1, n_sta):
            for part in range(2):
                spectra_copy(c, k, part).wait_send()
        for part in range(2):
            for o in range(n_sta):
                far, near, is_me = box_copies(c, o, part)
                pl.when(jnp.logical_not(is_me))(lambda far=far: far().wait_send())
    for k in range(1, n_sta):
        label_copy(k).wait_send()


def by_frequency(spectra, pair_bins, owner_count, bin_order):
    n_sta, n_win = lax.axis_size("sta"), lax.axis_size("win")
    windows, stations, columns = spectra.shape
    rounds = pair_bins.shape[1]
    width = columns // 2
    share = width // n_sta
    chunks = share // LANES
    out_cols = columns // n_win
    per_out = out_cols // share
    depth = -(-rounds * ROWS * ROWS // LANES) * LANES
    sizes = (n_sta, n_win, chunks, windows, stations, rounds, width)
    dma = pltpu.SemaphoreType.DMA
    sums = pl.pallas_call(
        functools.partial(kernel, sizes),
        out_shape=jax.ShapeDtypeStruct((CAP, out_cols), jnp.float32),
        in_specs=[
            pl.BlockSpec(memory_space=pl.ANY),
            pl.BlockSpec(memory_space=pltpu.SMEM),
            pl.BlockSpec(memory_space=pltpu.SMEM),
            pl.BlockSpec(memory_space=pltpu.SMEM),
        ],
        out_specs=pl.BlockSpec(memory_space=pltpu.VMEM),
        scratch_shapes=[
            pltpu.VMEM((chunks, n_sta, 2, stations, windows, LANES), spectra.dtype),
            pltpu.VMEM((n_sta, 2, windows * ROWS, LANES), jnp.float32),
            pltpu.VMEM((n_sta, 1, depth), jnp.int32),
            pltpu.VMEM((n_sta * CAP, LANES), jnp.int32),
            pltpu.VMEM((depth, 2 * LANES), jnp.bfloat16),
            pltpu.VMEM((n_sta * CAP, 2 * LANES), jnp.float32),
            pltpu.VMEM((chunks, 2, n_sta, CAP, LANES), jnp.float32),
            pltpu.VMEM((n_win, CAP, out_cols), jnp.float32),
            dma((chunks, n_sta, 2)),
            dma((chunks, n_sta, 2)),
            dma((chunks, 2)),
            dma((n_sta,)),
            dma((n_sta,)),
            dma((chunks, 2, n_sta)),
            dma((chunks, per_out, n_win)),
        ],
        compiler_params=pltpu.CompilerParams(
            collective_id=0, has_side_effects=True, vmem_limit_bytes=56 * 1024 * 1024
        ),
        cost_estimate=pl.CostEstimate(
            flops=8 * width * windows * rounds * stations * stations,
            bytes_accessed=2 * spectra.size, transcendentals=0,
        ),
    )(jnp.transpose(spectra, (1, 0, 2)), jnp.transpose(pair_bins, (1, 0, 2)), owner_count, bin_order)
    return sums * jnp.float32(1.0 / (windows * n_win))


def on_device(spectra, pair_bins, owner_count, bin_order):
    n_sta, n_win = lax.axis_size("sta"), lax.axis_size("win")
    width = spectra.shape[2] // 2
    share, out_cols = width // n_sta, 2 * width // n_win
    fits = (
        width % (n_sta * LANES) == 0 and out_cols % share == 0 and width % out_cols == 0
        and spectra.shape[1] <= ROWS and pair_bins.shape[1] <= n_sta - 1
    )
    plan = by_frequency if fits else by_blocks
    return plan(spectra, pair_bins, owner_count, bin_order)


def solution(mesh):
    return jax.shard_map(
        on_device,
        mesh=mesh,
        in_specs=(P("win", "sta", None), P("sta", None, None), P(), P()),
        out_specs=P("sta", "win"),
        check_vma=False,
    )
```

profile of v0, /device:TPU:1, one launch (start us, length us, event | category | flops | bytes accessed | tf_op | source)
XLA Modules:
  0.0 46.2 jit_solution(1418056564714921093)
XLA Ops:
  0.0 44.8 %shard_map.46 = f32[4,1024]{1,0:T(4,128)} custom-call(bf16[7,16,4096]{2,1,0:T(8,128)(2,1)} %bitcast.2, s32[3,7,7]{2,1,0:T(8,128)} %bitcast.3, s32[8]{0:T(128)} %count_ref.1, s32[16]{0:T(128)} %order_ref.1), custom_call_target="tpu_custom_call" | custom-call | flops 38535168 | bytes 917504 | tf_op jit(solution)/shard_map/pallas_call | solution.py:271
  44.8 1.3 %broadcast_multiply_fusion = f32[4,1024]{1,0:T(4,128)} fusion(f32[4,1024]{1,0:T(4,128)} %shard_map.46), kind=kLoop, calls=%fused_computation | loop fusion | flops 4096 | bytes 32768 | tf_op jit(solution)/shard_map/mul | solution.py:306
where the time goes:
time: 46.4 us; the launch traced here: 46.2 us
  Pallas kernels  44.8 us (97%)
  other arithmetic  1.33 us (3%)
    pallas_call x1, Pallas kernels, by_frequency(): pl.pallas_call(functools.partial(kernel, sizes), out_shape=jax.ShapeDtype...  44.8 us
    mul x1, other arithmetic, by_frequency(): return sums * jnp.float32(1.0 / (windows * n_win))  1.33 us

commit v1 on v0

--- a/solution.py
+++ b/solution.py
@@ -76,12 +76,26 @@
         )
     pl.semaphore_wait(barrier, n_sta * n_win - 1)
 
+    def partner(k):
+        if n_sta & (n_sta - 1):
+            return lax.rem(me + k, n_sta)
+        digits, bit = me, 1
+        while bit < n_sta:
+            if k & bit:
+                digits = digits + bit - 2 * bit * lax.rem(digits // bit, 2)
+            bit *= 2
+        return digits
+
+    far_half = list(range(n_sta // 2, n_sta))
+    near_half = list(range(1, n_sta // 2)) + [None]
+    turns = [k for pair in zip(far_half, near_half) for k in pair if k is not None]
+
     def share_of(dest, c, part):
         col = pl.multiple_of(part * width + dest * share + c * LANES, LANES)
         return spec_ref.at[:, :, pl.ds(col, LANES)]
 
     def spectra_copy(c, k, part):
-        dest = lax.rem(me + k, n_sta)
+        dest = partner(k)
         return pltpu.make_async_remote_copy(
             src_ref=share_of(dest, c, part),
             dst_ref=recv.at[c, me, part],
@@ -95,11 +109,11 @@
         return pltpu.make_async_copy(share_of(me, c, part), recv.at[c, me, part], own_sem.at[c, part])
 
     for c in range(chunks):
-        for k in range(1, n_sta):
-            for part in range(2):
-                spectra_copy(c, k, part).start()
         for part in range(2):
             own_copy(c, part).start()
+    for k in turns:
+        for part in range(2):
+            spectra_copy(0, k, part).start()
 
     lane = lax.broadcasted_iota(jnp.int32, (1, lab.shape[2]), 1)
     row = jnp.full((1, lab.shape[2]), -2, jnp.int32)
@@ -142,6 +156,12 @@
             recv_sem=lab_recv.at[src], device_id=(src, g), device_id_type=MESH,
         ).wait_recv()
 
+    for c in range(1, chunks):
+        for k in turns:
+            for part in range(2):
+                spectra_copy(c - 1, k, part).wait_send()
+                spectra_copy(c, k, part).start()
+
     def widen(c, p):
         for part in range(2):
             for j in range(stations):
@@ -161,20 +181,22 @@
         blocks = [lax.rem(p + r, n_sta) for r in range(rounds)]
         re = [[None] * stations for _ in range(rounds)]
         im = [[None] * stations for _ in range(rounds)]
-        for w in range(windows):
-            at = pl.ds(w * ROWS, ROWS)
-            mine = [(wide[b, 0, at, :], wide[b, 1, at, :]) for b in blocks]
-            for j in range(stations):
-                a = jnp.broadcast_to(wide[p, 0, pl.ds(w * ROWS + j, 1), :], (ROWS, LANES))
-                b = jnp.broadcast_to(wide[p, 1, pl.ds(w * ROWS + j, 1), :], (ROWS, LANES))
-                for r in range(rounds):
-                    x, y = mine[r]
-                    if w == 0:
-                        re[r][j] = x * a + y * b
-                        im[r][j] = y * a - x * b
-                    else:
-                        re[r][j] = re[r][j] + x * a + y * b
-                        im[r][j] = im[r][j] + y * a - x * b
+        half = -(-stations // 2)
+        for group in (range(half), range(half, stations)):
+            for w in range(windows):
+                at = pl.ds(w * ROWS, ROWS)
+                mine = [(wide[b, 0, at, :], wide[b, 1, at, :]) for b in blocks]
+                for j in group:
+                    a = wide[p, 0, pl.ds(w * ROWS + j, ROWS, stride=0), :]
+                    b = wide[p, 1, pl.ds(w * ROWS + j, ROWS, stride=0), :]
+                    for r in range(rounds):
+                        x, y = mine[r]
+                        if w == 0:
+                            re[r][j] = x * a + y * b
+                            im[r][j] = y * a - x * b
+                        else:
+                            re[r][j] = re[r][j] + x * a + y * b
+                            im[r][j] = im[r][j] + y * a - x * b
         blank = jnp.zeros((ROWS, LANES), jnp.float32)
         for r in range(rounds):
             at = pl.ds(r * ROWS * ROWS, ROWS * ROWS)
@@ -244,10 +266,10 @@
                 pltpu.make_async_copy(dst, dst, box_recv.at[c, t, s]).wait()
     out_ref[...] = functools.reduce(jnp.add, [inbox[s] for s in range(n_win)])
 
+    for k in turns:
+        for part in range(2):
+            spectra_copy(chunks - 1, k, part).wait_send()
     for c in range(chunks):
-        for k in range(1, n_sta):
-            for part in range(2):
-                spectra_copy(c, k, part).wait_send()
         for part in range(2):
             for o in range(n_sta):
                 far, near, is_me = box_copies(c, o, part)

time: 46.4 us -> 43.1 us (0.929)
  Pallas kernels: 44.8 us -> 41.5 us
    pallas_call x1, Pallas kernels: 44.8 us -> 41.5 us  [by_frequency(): pl.pallas_call(functools.partial(kernel, sizes), out_shape=jax.ShapeDtype...]
where the time goes in v1:
time: 43.1 us; the launch traced here: 42.8 us
  Pallas kernels  41.5 us (96%)
  other arithmetic  1.33 us (3%)
    pallas_call x1, Pallas kernels, by_frequency(): pl.pallas_call(functools.partial(kernel, sizes), out_shape=jax.ShapeDtype...  41.5 us
    mul x1, other arithmetic, by_frequency(): return sums * jnp.float32(1.0 / (windows * n_win))  1.33 us

profile of v1, /device:TPU:1, one launch (start us, length us, event | category | flops | bytes accessed | tf_op | source)
XLA Modules:
  0.0 42.8 jit_solution(11547053296287101567)
XLA Ops:
  0.0 41.5 %shard_map.46 = f32[4,1024]{1,0:T(4,128)} custom-call(bf16[7,16,4096]{2,1,0:T(8,128)(2,1)} %bitcast.2, s32[3,7,7]{2,1,0:T(8,128)} %bitcast.3, s32[8]{0:T(128)} %count_ref.1, s32[16]{0:T(128)} %order_ref.1), custom_call_target="tpu_custom_call" | custom-call | flops 38535168 | bytes 917504 | tf_op jit(solution)/shard_map/pallas_call | solution.py:293
  41.5 1.3 %broadcast_multiply_fusion = f32[4,1024]{1,0:T(4,128)} fusion(f32[4,1024]{1,0:T(4,128)} %shard_map.46), kind=kLoop, calls=%fused_computation | loop fusion | flops 4096 | bytes 32768 | tf_op jit(solution)/shard_map/mul | solution.py:328

commit v2 on v1

--- a/solution.py
+++ b/solution.py
@@ -148,7 +148,6 @@
     slots[...] = slot
 
     wide[...] = jnp.zeros_like(wide)
-    crossed[...] = jnp.zeros_like(crossed)
     for k in range(1, n_sta):
         src = lax.rem(me - k + n_sta, n_sta)
         pltpu.make_async_remote_copy(
@@ -177,7 +176,7 @@
             ).wait_recv()
         widen(c, src)
 
-    def step(p):
+    def step(p, at_buffer):
         blocks = [lax.rem(p + r, n_sta) for r in range(rounds)]
         re = [[None] * stations for _ in range(rounds)]
         im = [[None] * stations for _ in range(rounds)]
@@ -201,8 +200,11 @@
         for r in range(rounds):
             at = pl.ds(r * ROWS * ROWS, ROWS * ROWS)
             pad = [blank] * (ROWS - stations)
-            crossed[at, 0:LANES] = jnp.concatenate(re[r] + pad, axis=0).astype(jnp.bfloat16)
-            crossed[at, LANES:] = jnp.concatenate(im[r] + pad, axis=0).astype(jnp.bfloat16)
+            crossed[at_buffer, at, 0:LANES] = jnp.concatenate(re[r] + pad, axis=0).astype(jnp.bfloat16)
+            crossed[at_buffer, at, LANES:] = jnp.concatenate(im[r] + pad, axis=0).astype(jnp.bfloat16)
+
+    def binned(p, at_buffer):
+        blocks = [lax.rem(p + r, n_sta) for r in range(rounds)]
         lanes = lax.broadcasted_iota(jnp.int32, (1, lab.shape[2]), 1)
         names = jnp.full((1, lab.shape[2]), -2, jnp.int32)
         for r in range(rounds):
@@ -211,7 +213,7 @@
             [slots[...] == names[:, at:at + LANES] for at in range(0, lab.shape[2], LANES)], axis=1
         )
         match = jnp.where(match, 1.0, 0.0).astype(jnp.bfloat16)
-        return jnp.dot(match, crossed[...], preferred_element_type=jnp.float32)
+        return jnp.dot(match, crossed[at_buffer], preferred_element_type=jnp.float32)
 
     def box_copies(c, o, part):
         q = part * halves + me // per_out
@@ -237,16 +239,21 @@
         widen(c, me)
         arrive(c, 1)
         total[...] = jnp.zeros_like(total)
+        crossed[...] = jnp.zeros_like(crossed)
 
         def one_step(k, carry):
             @pl.when(k < n_sta)
             def _():
                 arrive(c, k)
 
-            total[...] += step(lax.rem(me - k + 2 * n_sta, n_sta))
+            now = lax.rem(k, 2)
+            total[...] += binned(lax.rem(me - k + 1 + 2 * n_sta, n_sta), 1 - now)
+            step(lax.rem(me - k + 2 * n_sta, n_sta), now)
             return carry
 
-        lax.fori_loop(rounds - 1, n_sta + rounds - 1, one_step, 0)
+        last = n_sta + rounds - 1
+        lax.fori_loop(rounds - 1, last, one_step, 0)
+        total[...] += binned(lax.rem(me - last + 1 + 2 * n_sta, n_sta), (last - 1) % 2)
         for part in range(2):
             for o in range(n_sta):
                 outbox[c, part, o] = total[o * CAP:(o + 1) * CAP, part * LANES:(part + 1) * LANES]
@@ -305,7 +312,7 @@
             pltpu.VMEM((n_sta, 2, windows * ROWS, LANES), jnp.float32),
             pltpu.VMEM((n_sta, 1, depth), jnp.int32),
             pltpu.VMEM((n_sta * CAP, LANES), jnp.int32),
-            pltpu.VMEM((depth, 2 * LANES), jnp.bfloat16),
+            pltpu.VMEM((2, depth, 2 * LANES), jnp.bfloat16),
             pltpu.VMEM((n_sta * CAP, 2 * LANES), jnp.float32),
             pltpu.VMEM((chunks, 2, n_sta, CAP, LANES), jnp.float32),
             pltpu.VMEM((n_win, CAP, out_cols), jnp.float32),

time: 43.1 us -> 42.8 us (level)
  no operation moved by 1% of the time
where the time goes in v2:
time: 42.8 us; the launch traced here: 42.5 us
  Pallas kernels  41.2 us (96%)
  other arithmetic  1.33 us (3%)
    pallas_call x1, Pallas kernels, by_frequency(): pl.pallas_call(functools.partial(kernel, sizes), out_shape=jax.ShapeDtype...  41.2 us
    mul x1, other arithmetic, by_frequency(): return sums * jnp.float32(1.0 / (windows * n_win))  1.33 us

profile of v2, /device:TPU:1, one launch (start us, length us, event | category | flops | bytes accessed | tf_op | source)
XLA Modules:
  0.0 42.5 jit_solution(8586583180588520838)
XLA Ops:
  0.0 41.2 %shard_map.46 = f32[4,1024]{1,0:T(4,128)} custom-call(bf16[7,16,4096]{2,1,0:T(8,128)(2,1)} %bitcast.2, s32[3,7,7]{2,1,0:T(8,128)} %bitcast.3, s32[8]{0:T(128)} %count_ref.1, s32[16]{0:T(128)} %order_ref.1), custom_call_target="tpu_custom_call" | custom-call | flops 38535168 | bytes 917504 | tf_op jit(solution)/shard_map/pallas_call | solution.py:300
  41.2 1.3 %broadcast_multiply_fusion = f32[4,1024]{1,0:T(4,128)} fusion(f32[4,1024]{1,0:T(4,128)} %shard_map.46), kind=kLoop, calls=%fused_computation | loop fusion | flops 4096 | bytes 32768 | tf_op jit(solution)/shard_map/mul | solution.py:335

commit v3 on v2

--- a/solution.py
+++ b/solution.py
@@ -69,12 +69,15 @@
     g = lax.axis_index("win")
 
     barrier = pltpu.get_barrier_semaphore()
-    for t in range(1, n_sta * n_win):
-        flat = lax.rem(me * n_win + g + t, n_sta * n_win)
+    for t in range(1, n_sta):
         pl.semaphore_signal(
-            barrier, inc=1, device_id=(flat // n_win, lax.rem(flat, n_win)), device_id_type=MESH
-        )
-    pl.semaphore_wait(barrier, n_sta * n_win - 1)
+            barrier, inc=1, device_id=(lax.rem(me + t, n_sta), g), device_id_type=MESH
+        )
+    for t in range(1, n_win):
+        pl.semaphore_signal(
+            barrier, inc=1, device_id=(me, lax.rem(g + t, n_win)), device_id_type=MESH
+        )
+    pl.semaphore_wait(barrier, n_sta + n_win - 2)
 
     def partner(k):
         if n_sta & (n_sta - 1):
@@ -301,7 +304,7 @@
         functools.partial(kernel, sizes),
         out_shape=jax.ShapeDtypeStruct((CAP, out_cols), jnp.float32),
         in_specs=[
-            pl.BlockSpec(memory_space=pl.ANY),
+            pl.BlockSpec(memory_space=pltpu.VMEM),
             pl.BlockSpec(memory_space=pltpu.SMEM),
             pl.BlockSpec(memory_space=pltpu.SMEM),
             pl.BlockSpec(memory_space=pltpu.SMEM),

time: 42.8 us -> 42 us (0.981)
  Pallas kernels: 41.2 us -> 40.4 us
    pallas_call x1, Pallas kernels: 41.2 us -> 40.4 us  [by_frequency(): pl.pallas_call(functools.partial(kernel, sizes), out_shape=jax.ShapeDtype...]
where the time goes in v3:
time: 42 us; the launch traced here: 41.7 us
  Pallas kernels  40.4 us (96%)
  other arithmetic  1.33 us (3%)
    pallas_call x1, Pallas kernels, by_frequency(): pl.pallas_call(functools.partial(kernel, sizes), out_shape=jax.ShapeDtype...  40.4 us
    mul x1, other arithmetic, by_frequency(): return sums * jnp.float32(1.0 / (windows * n_win))  1.33 us

profile of v3, /device:TPU:1, one launch (start us, length us, event | category | flops | bytes accessed | tf_op | source)
XLA Modules:
  0.0 41.7 jit_solution(12956102930129250774)
XLA Ops:
  0.0 40.4 %shard_map.46 = f32[4,1024]{1,0:T(4,128)} custom-call(bf16[7,16,4096]{2,1,0:T(8,128)(2,1)} %bitcast.2, s32[3,7,7]{2,1,0:T(8,128)} %bitcast.3, s32[8]{0:T(128)} %count_ref.1, s32[16]{0:T(128)} %order_ref.1), custom_call_target="tpu_custom_call" | custom-call | flops 38535168 | bytes 917504 | tf_op jit(solution)/shard_map/pallas_call | solution.py:303
  40.4 1.3 %broadcast_multiply_fusion = f32[4,1024]{1,0:T(4,128)} fusion(f32[4,1024]{1,0:T(4,128)} %shard_map.46), kind=kLoop, calls=%fused_computation | loop fusion | flops 4096 | bytes 32768 | tf_op jit(solution)/shard_map/mul | solution.py:338

commit v4 on v2

--- a/solution.py
+++ b/solution.py
@@ -57,8 +57,8 @@
 
 def kernel(
     sizes, spec_ref, bins_ref, count_ref, order_ref, out_ref,
-    recv, wide, lab, slots, crossed, total, outbox, inbox,
-    send_sem, recv_sem, own_sem, lab_send, lab_recv, box_send, box_recv,
+    stage, recv, wide, lab, slots, crossed, total, outbox, inbox,
+    stage_sem, send_sem, recv_sem, own_sem, lab_send, lab_recv, box_send, box_recv,
 ):
     n_sta, n_win, chunks, windows, stations, rounds, width = sizes
     share = width // n_sta
@@ -67,14 +67,6 @@
     halves = width // out_cols
     me = lax.axis_index("sta")
     g = lax.axis_index("win")
-
-    barrier = pltpu.get_barrier_semaphore()
-    for t in range(1, n_sta * n_win):
-        flat = lax.rem(me * n_win + g + t, n_sta * n_win)
-        pl.semaphore_signal(
-            barrier, inc=1, device_id=(flat // n_win, lax.rem(flat, n_win)), device_id_type=MESH
-        )
-    pl.semaphore_wait(barrier, n_sta * n_win - 1)
 
     def partner(k):
         if n_sta & (n_sta - 1):
@@ -94,26 +86,44 @@
         col = pl.multiple_of(part * width + dest * share + c * LANES, LANES)
         return spec_ref.at[:, :, pl.ds(col, LANES)]
 
-    def spectra_copy(c, k, part):
-        dest = partner(k)
-        return pltpu.make_async_remote_copy(
-            src_ref=share_of(dest, c, part),
-            dst_ref=recv.at[c, me, part],
-            send_sem=send_sem.at[c, k, part],
-            recv_sem=recv_sem.at[c, me, part],
-            device_id=(dest, g),
-            device_id_type=MESH,
-        )
+    def stage_copy(c, k, part):
+        return pltpu.make_async_copy(share_of(partner(k), c, part), stage.at[c, k, part], stage_sem.at[c, k, part])
 
     def own_copy(c, part):
         return pltpu.make_async_copy(share_of(me, c, part), recv.at[c, me, part], own_sem.at[c, part])
 
+    def spectra_copy(c, k):
+        return pltpu.make_async_remote_copy(
+            src_ref=stage.at[c, k],
+            dst_ref=recv.at[c, me],
+            send_sem=send_sem.at[c, k],
+            recv_sem=recv_sem.at[c, me],
+            device_id=(partner(k), g),
+            device_id_type=MESH,
+        )
+
     for c in range(chunks):
+        for k in turns:
+            for part in range(2):
+                stage_copy(c, k, part).start()
         for part in range(2):
             own_copy(c, part).start()
+
+    barrier = pltpu.get_barrier_semaphore()
+    for t in range(1, n_sta):
+        pl.semaphore_signal(
+            barrier, inc=1, device_id=(lax.rem(me + t, n_sta), g), device_id_type=MESH
+        )
+    for t in range(1, n_win):
+        pl.semaphore_signal(
+            barrier, inc=1, device_id=(me, lax.rem(g + t, n_win)), device_id_type=MESH
+        )
+    pl.semaphore_wait(barrier, n_sta + n_win - 2)
+
     for k in turns:
         for part in range(2):
-            spectra_copy(0, k, part).start()
+            stage_copy(0, k, part).wait()
+        spectra_copy(0, k).start()
 
     lane = lax.broadcasted_iota(jnp.int32, (1, lab.shape[2]), 1)
     row = jnp.full((1, lab.shape[2]), -2, jnp.int32)
@@ -158,8 +168,9 @@
     for c in range(1, chunks):
         for k in turns:
             for part in range(2):
-                spectra_copy(c - 1, k, part).wait_send()
-                spectra_copy(c, k, part).start()
+                stage_copy(c, k, part).wait()
+            spectra_copy(c - 1, k).wait_send()
+            spectra_copy(c, k).start()
 
     def widen(c, p):
         for part in range(2):
@@ -168,12 +179,11 @@
 
     def arrive(c, k):
         src = lax.rem(me - k + n_sta, n_sta)
-        for part in range(2):
-            pltpu.make_async_remote_copy(
-                src_ref=recv.at[c, src, part], dst_ref=recv.at[c, src, part],
-                send_sem=send_sem.at[c, k, part], recv_sem=recv_sem.at[c, src, part],
-                device_id=(src, g), device_id_type=MESH,
-            ).wait_recv()
+        pltpu.make_async_remote_copy(
+            src_ref=recv.at[c, src], dst_ref=recv.at[c, src],
+            send_sem=send_sem.at[c, k], recv_sem=recv_sem.at[c, src],
+            device_id=(src, g), device_id_type=MESH,
+        ).wait_recv()
         widen(c, src)
 
     def step(p, at_buffer):
@@ -274,8 +284,7 @@
     out_ref[...] = functools.reduce(jnp.add, [inbox[s] for s in range(n_win)])
 
     for k in turns:
-        for part in range(2):
-            spectra_copy(chunks - 1, k, part).wait_send()
+        spectra_copy(chunks - 1, k).wait_send()
     for c in range(chunks):
         for part in range(2):
             for o in range(n_sta):
@@ -309,6 +318,7 @@
         out_specs=pl.BlockSpec(memory_space=pltpu.VMEM),
         scratch_shapes=[
             pltpu.VMEM((chunks, n_sta, 2, stations, windows, LANES), spectra.dtype),
+            pltpu.VMEM((chunks, n_sta, 2, stations, windows, LANES), spectra.dtype),
             pltpu.VMEM((n_sta, 2, windows * ROWS, LANES), jnp.float32),
             pltpu.VMEM((n_sta, 1, depth), jnp.int32),
             pltpu.VMEM((n_sta * CAP, LANES), jnp.int32),
@@ -317,7 +327,8 @@
             pltpu.VMEM((chunks, 2, n_sta, CAP, LANES), jnp.float32),
             pltpu.VMEM((n_win, CAP, out_cols), jnp.float32),
             dma((chunks, n_sta, 2)),
-            dma((chunks, n_sta, 2)),
+            dma((chunks, n_sta)),
+            dma((chunks, n_sta)),
             dma((chunks, 2)),
             dma((n_sta,)),
             dma((n_sta,)),

time: 42.8 us -> 41.7 us (0.974)
  Pallas kernels: 41.2 us -> 40.1 us
    pallas_call x1, Pallas kernels: 41.2 us -> 40.1 us  [by_frequency(): pl.pallas_call(functools.partial(kernel, sizes), out_shape=jax.ShapeDtype...]
where the time goes in v4:
time: 41.7 us; the launch traced here: 41.5 us
  Pallas kernels  40.1 us (96%)
  other arithmetic  1.33 us (3%)
    pallas_call x1, Pallas kernels, by_frequency(): pl.pallas_call(functools.partial(kernel, sizes), out_shape=jax.ShapeDtype...  40.1 us
    mul x1, other arithmetic, by_frequency(): return sums * jnp.float32(1.0 / (windows * n_win))  1.33 us

profile of v4, /device:TPU:1, one launch (start us, length us, event | category | flops | bytes accessed | tf_op | source)
XLA Modules:
  0.0 41.5 jit_solution(13403381821271896221)
XLA Ops:
  0.0 40.1 %shard_map.46 = f32[4,1024]{1,0:T(4,128)} custom-call(bf16[7,16,4096]{2,1,0:T(8,128)(2,1)} %bitcast.2, s32[3,7,7]{2,1,0:T(8,128)} %bitcast.3, s32[8]{0:T(128)} %count_ref.1, s32[16]{0:T(128)} %order_ref.1), custom_call_target="tpu_custom_call" | custom-call | flops 38535168 | bytes 917504 | tf_op jit(solution)/shard_map/pallas_call | solution.py:309
  40.2 1.3 %broadcast_multiply_fusion = f32[4,1024]{1,0:T(4,128)} fusion(f32[4,1024]{1,0:T(4,128)} %shard_map.46), kind=kLoop, calls=%fused_computation | loop fusion | flops 4096 | bytes 32768 | tf_op jit(solution)/shard_map/mul | solution.py:346

commit v5 on v4

--- a/solution.py
+++ b/solution.py
@@ -118,13 +118,6 @@
         pl.semaphore_signal(
             barrier, inc=1, device_id=(me, lax.rem(g + t, n_win)), device_id_type=MESH
         )
-    pl.semaphore_wait(barrier, n_sta + n_win - 2)
-
-    for k in turns:
-        for part in range(2):
-            stage_copy(0, k, part).wait()
-        spectra_copy(0, k).start()
-
     lane = lax.broadcasted_iota(jnp.int32, (1, lab.shape[2]), 1)
     row = jnp.full((1, lab.shape[2]), -2, jnp.int32)
     for r in range(rounds):
@@ -132,19 +125,6 @@
             for i in range(stations):
                 row = jnp.where(lane == (r * ROWS + j) * ROWS + i, bins_ref[r, i, j], row)
     lab[pl.ds(me, 1)] = row[None]
-
-    def label_copy(k):
-        return pltpu.make_async_remote_copy(
-            src_ref=lab.at[me],
-            dst_ref=lab.at[me],
-            send_sem=lab_send.at[k],
-            recv_sem=lab_recv.at[me],
-            device_id=(lax.rem(me + k, n_sta), g),
-            device_id_type=MESH,
-        )
-
-    for k in range(1, n_sta):
-        label_copy(k).start()
 
     sub = lax.broadcasted_iota(jnp.int32, (n_sta * CAP, LANES), 0)
     slot = jnp.full((n_sta * CAP, LANES), -1, jnp.int32)
@@ -158,6 +138,33 @@
     slots[...] = slot
 
     wide[...] = jnp.zeros_like(wide)
+    pl.semaphore_wait(barrier, n_sta + n_win - 2)
+
+    def label_copy(k):
+        return pltpu.make_async_remote_copy(
+            src_ref=lab.at[me],
+            dst_ref=lab.at[me],
+            send_sem=lab_send.at[k],
+            recv_sem=lab_recv.at[me],
+            device_id=(lax.rem(me + k, n_sta), g),
+            device_id_type=MESH,
+        )
+
+    for k in range(1, n_sta):
+        label_copy(k).start()
+
+    for k in turns:
+        for part in range(2):
+            stage_copy(0, k, part).wait()
+        spectra_copy(0, k).start()
+
+    for c in range(1, chunks):
+        for k in turns:
+            for part in range(2):
+                stage_copy(c, k, part).wait()
+            spectra_copy(c - 1, k).wait_send()
+            spectra_copy(c, k).start()
+
     for k in range(1, n_sta):
         src = lax.rem(me - k + n_sta, n_sta)
         pltpu.make_async_remote_copy(
@@ -165,26 +172,20 @@
             recv_sem=lab_recv.at[src], device_id=(src, g), device_id_type=MESH,
         ).wait_recv()
 
-    for c in range(1, chunks):
-        for k in turns:
-            for part in range(2):
-                stage_copy(c, k, part).wait()
-            spectra_copy(c - 1, k).wait_send()
-            spectra_copy(c, k).start()
-
     def widen(c, p):
         for part in range(2):
             for j in range(stations):
                 wide[p, part, pl.ds(j, windows, stride=ROWS), :] = recv[c, p, part, j].astype(jnp.float32)
 
-    def arrive(c, k):
-        src = lax.rem(me - k + n_sta, n_sta)
-        pltpu.make_async_remote_copy(
-            src_ref=recv.at[c, src], dst_ref=recv.at[c, src],
-            send_sem=send_sem.at[c, k], recv_sem=recv_sem.at[c, src],
-            device_id=(src, g), device_id_type=MESH,
-        ).wait_recv()
-        widen(c, src)
+    def arrive(c, src):
+        @pl.when(src != me)
+        def _():
+            pltpu.make_async_remote_copy(
+                src_ref=recv.at[c, src], dst_ref=recv.at[c, src],
+                send_sem=send_sem.at[c, 0], recv_sem=recv_sem.at[c, src],
+                device_id=(src, g), device_id_type=MESH,
+            ).wait_recv()
+            widen(c, src)
 
     def step(p, at_buffer):
         blocks = [lax.rem(p + r, n_sta) for r in range(rounds)]
@@ -225,7 +226,8 @@
         match = jnp.where(match, 1.0, 0.0).astype(jnp.bfloat16)
         return jnp.dot(match, crossed[at_buffer], preferred_element_type=jnp.float32)
 
-    def box_copies(c, o, part):
+    def box_copies(c, k, part):
+        o = partner(k)
         q = part * halves + me // per_out
         t = lax.rem(me, per_out)
         col = pl.multiple_of(t * share + c * LANES, LANES)
@@ -234,44 +236,58 @@
 
         def far():
             return pltpu.make_async_remote_copy(
-                src_ref=src, dst_ref=dst, send_sem=box_send.at[c, part, o],
+                src_ref=src, dst_ref=dst, send_sem=box_send.at[c, part, k],
                 recv_sem=box_recv.at[c, t, g], device_id=(o, q), device_id_type=MESH,
             )
 
         def near():
             return pltpu.make_async_copy(src, dst, box_recv.at[c, t, g])
 
-        return far, near, jnp.logical_and(o == me, q == g)
+        return far, near, q == g
+
+    quarter = n_sta // 4
+    place = lax.rem(me, 2 * quarter) // quarter * 2 + lax.rem(me, 2)
+    low = me // (n_sta // 2) * (n_sta // 2)
+    way = jnp.where(place == 3, -1, 1)
+    first = low + jnp.where(place == 3, 1, jnp.where(place == 2, n_sta - 2, 0))
+
+    def block_at(t):
+        return lax.rem(first + way * t + 2 * n_sta, n_sta)
 
     def one_chunk(c, carry):
         for part in range(2):
             own_copy(c, part).wait()
         widen(c, me)
-        arrive(c, 1)
+        for r in range(rounds - 1):
+            arrive(c, lax.rem(block_at(0) + r + jnp.where(way < 0, 1, 0), n_sta))
         total[...] = jnp.zeros_like(total)
         crossed[...] = jnp.zeros_like(crossed)
 
-        def one_step(k, carry):
-            @pl.when(k < n_sta)
+        def one_step(t, carry):
+            p = block_at(t)
+
+            @pl.when(t <= n_sta - rounds)
             def _():
-                arrive(c, k)
-
-            now = lax.rem(k, 2)
-            total[...] += binned(lax.rem(me - k + 1 + 2 * n_sta, n_sta), 1 - now)
-            step(lax.rem(me - k + 2 * n_sta, n_sta), now)
+                arrive(c, lax.rem(p + jnp.where(way < 0, 0, rounds - 1), n_sta))
+
+            now = lax.rem(t, 2)
+            total[...] += binned(block_at(t - 1), 1 - now)
+            step(p, now)
             return carry
 
-        last = n_sta + rounds - 1
-        lax.fori_loop(rounds - 1, last, one_step, 0)
-        total[...] += binned(lax.rem(me - last + 1 + 2 * n_sta, n_sta), (last - 1) % 2)
+        lax.fori_loop(0, n_sta, one_step, 0)
+        total[...] += binned(block_at(n_sta - 1), (n_sta - 1) % 2)
         for part in range(2):
             for o in range(n_sta):
                 outbox[c, part, o] = total[o * CAP:(o + 1) * CAP, part * LANES:(part + 1) * LANES]
         for part in range(2):
-            for o in range(n_sta):
-                far, near, is_me = box_copies(c, o, part)
-                pl.when(is_me)(lambda near=near: near().start())
-                pl.when(jnp.logical_not(is_me))(lambda far=far: far().start())
+            for k in range(n_sta):
+                far, near, is_me = box_copies(c, k, part)
+                if k:
+                    far().start()
+                else:
+                    pl.when(is_me)(lambda near=near: near().start())
+                    pl.when(jnp.logical_not(is_me))(lambda far=far: far().start())
         return carry
 
     lax.fori_loop(0, chunks, one_chunk, 0)
@@ -287,9 +303,12 @@
         spectra_copy(chunks - 1, k).wait_send()
     for c in range(chunks):
         for part in range(2):
-            for o in range(n_sta):
-                far, near, is_me = box_copies(c, o, part)
-                pl.when(jnp.logical_not(is_me))(lambda far=far: far().wait_send())
+            for k in range(n_sta):
+                far, near, is_me = box_copies(c, k, part)
+                if k:
+                    far().wait_send()
+                else:
+                    pl.when(jnp.logical_not(is_me))(lambda far=far: far().wait_send())
     for k in range(1, n_sta):
         label_copy(k).wait_send()
 

time: 41.7 us -> 38.8 us (0.930)
  Pallas kernels: 40.1 us -> 37.2 us
    pallas_call x1, Pallas kernels: 40.1 us -> 37.2 us  [by_frequency(): pl.pallas_call(functools.partial(kernel, sizes), out_shape=jax.ShapeDtype...]
where the time goes in v5:
time: 38.8 us; the launch traced here: 38.5 us
  Pallas kernels  37.2 us (96%)
  other arithmetic  1.33 us (3%)
    pallas_call x1, Pallas kernels, by_frequency(): pl.pallas_call(functools.partial(kernel, sizes), out_shape=jax.ShapeDtype...  37.2 us
    mul x1, other arithmetic, by_frequency(): return sums * jnp.float32(1.0 / (windows * n_win))  1.33 us

profile of v5, /device:TPU:1, one launch (start us, length us, event | category | flops | bytes accessed | tf_op | source)
XLA Modules:
  0.0 38.5 jit_solution(11845935415500505114)
XLA Ops:
  0.0 37.2 %shard_map.46 = f32[4,1024]{1,0:T(4,128)} custom-call(bf16[7,16,4096]{2,1,0:T(8,128)(2,1)} %bitcast.2, s32[3,7,7]{2,1,0:T(8,128)} %bitcast.3, s32[8]{0:T(128)} %count_ref.1, s32[16]{0:T(128)} %order_ref.1), custom_call_target="tpu_custom_call" | custom-call | flops 38535168 | bytes 917504 | tf_op jit(solution)/shard_map/pallas_call | solution.py:328
  37.2 1.3 %broadcast_multiply_fusion = f32[4,1024]{1,0:T(4,128)} fusion(f32[4,1024]{1,0:T(4,128)} %shard_map.46), kind=kLoop, calls=%fused_computation | loop fusion | flops 4096 | bytes 32768 | tf_op jit(solution)/shard_map/mul | solution.py:365

commit v6 on v5

--- a/solution.py
+++ b/solution.py
@@ -162,7 +162,6 @@
         for k in turns:
             for part in range(2):
                 stage_copy(c, k, part).wait()
-            spectra_copy(c - 1, k).wait_send()
             spectra_copy(c, k).start()
 
     for k in range(1, n_sta):
@@ -299,8 +298,9 @@
                 pltpu.make_async_copy(dst, dst, box_recv.at[c, t, s]).wait()
     out_ref[...] = functools.reduce(jnp.add, [inbox[s] for s in range(n_win)])
 
-    for k in turns:
-        spectra_copy(chunks - 1, k).wait_send()
+    for c in range(chunks):
+        for k in turns:
+            spectra_copy(c, k).wait_send()
     for c in range(chunks):
         for part in range(2):
             for k in range(n_sta):

time: 38.8 us -> 38.8 us (level)
  no operation moved by 1% of the time
where the time goes in v6:
time: 38.8 us; the launch traced here: 38.5 us
  Pallas kernels  37.2 us (96%)
  other arithmetic  1.33 us (3%)
    pallas_call x1, Pallas kernels, by_frequency(): pl.pallas_call(functools.partial(kernel, sizes), out_shape=jax.ShapeDtype...  37.2 us
    mul x1, other arithmetic, by_frequency(): return sums * jnp.float32(1.0 / (windows * n_win))  1.33 us

profile of v6, /device:TPU:1, one launch (start us, length us, event | category | flops | bytes accessed | tf_op | source)
XLA Modules:
  0.0 38.5 jit_solution(17424977296180326310)
XLA Ops:
  0.0 37.2 %shard_map.46 = f32[4,1024]{1,0:T(4,128)} custom-call(bf16[7,16,4096]{2,1,0:T(8,128)(2,1)} %bitcast.2, s32[3,7,7]{2,1,0:T(8,128)} %bitcast.3, s32[8]{0:T(128)} %count_ref.1, s32[16]{0:T(128)} %order_ref.1), custom_call_target="tpu_custom_call" | custom-call | flops 38535168 | bytes 917504 | tf_op jit(solution)/shard_map/pallas_call | solution.py:328
  37.2 1.3 %broadcast_multiply_fusion = f32[4,1024]{1,0:T(4,128)} fusion(f32[4,1024]{1,0:T(4,128)} %shard_map.46), kind=kLoop, calls=%fused_computation | loop fusion | flops 4096 | bytes 32768 | tf_op jit(solution)/shard_map/mul | solution.py:365

commit v7 on v6

--- a/solution.py
+++ b/solution.py
@@ -172,9 +172,11 @@
         ).wait_recv()
 
     def widen(c, p):
-        for part in range(2):
-            for j in range(stations):
-                wide[p, part, pl.ds(j, windows, stride=ROWS), :] = recv[c, p, part, j].astype(jnp.float32)
+        for j in range(stations):
+            x = recv[c, p, 0, j].astype(jnp.float32)
+            y = recv[c, p, 1, j].astype(jnp.float32)
+            for part, value in enumerate((x, y, x + y, x - y)):
+                wide[p, part, pl.ds(j, windows, stride=ROWS), :] = value
 
     def arrive(c, src):
         @pl.when(src != me)
@@ -188,24 +190,25 @@
 
     def step(p, at_buffer):
         blocks = [lax.rem(p + r, n_sta) for r in range(rounds)]
-        re = [[None] * stations for _ in range(rounds)]
-        im = [[None] * stations for _ in range(rounds)]
+        both = [[None] * stations for _ in range(rounds)]
+        minus_re = [[None] * stations for _ in range(rounds)]
+        minus_im = [[None] * stations for _ in range(rounds)]
         half = -(-stations // 2)
         for group in (range(half), range(half, stations)):
             for w in range(windows):
                 at = pl.ds(w * ROWS, ROWS)
-                mine = [(wide[b, 0, at, :], wide[b, 1, at, :]) for b in blocks]
+                mine = [[wide[b, part, at, :] for part in range(3)] for b in blocks]
                 for j in group:
-                    a = wide[p, 0, pl.ds(w * ROWS + j, ROWS, stride=0), :]
-                    b = wide[p, 1, pl.ds(w * ROWS + j, ROWS, stride=0), :]
+                    a, a_plus_b, a_minus_b = [
+                        wide[p, part, pl.ds(w * ROWS + j, ROWS, stride=0), :] for part in (0, 2, 3)
+                    ]
                     for r in range(rounds):
-                        x, y = mine[r]
-                        if w == 0:
-                            re[r][j] = x * a + y * b
-                            im[r][j] = y * a - x * b
-                        else:
-                            re[r][j] = re[r][j] + x * a + y * b
-                            im[r][j] = im[r][j] + y * a - x * b
+                        x, y, x_plus_y = mine[r]
+                        terms = (a * x_plus_y, y * a_minus_b, x * a_plus_b)
+                        for sums, term in zip((both, minus_re, minus_im), terms):
+                            sums[r][j] = term if w == 0 else sums[r][j] + term
+        re = [[u - v for u, v in zip(both[r], minus_re[r])] for r in range(rounds)]
+        im = [[u - v for u, v in zip(both[r], minus_im[r])] for r in range(rounds)]
         blank = jnp.zeros((ROWS, LANES), jnp.float32)
         for r in range(rounds):
             at = pl.ds(r * ROWS * ROWS, ROWS * ROWS)
@@ -338,7 +341,7 @@
         scratch_shapes=[
             pltpu.VMEM((chunks, n_sta, 2, stations, windows, LANES), spectra.dtype),
             pltpu.VMEM((chunks, n_sta, 2, stations, windows, LANES), spectra.dtype),
-            pltpu.VMEM((n_sta, 2, windows * ROWS, LANES), jnp.float32),
+            pltpu.VMEM((n_sta, 4, windows * ROWS, LANES), jnp.float32),
             pltpu.VMEM((n_sta, 1, depth), jnp.int32),
             pltpu.VMEM((n_sta * CAP, LANES), jnp.int32),
             pltpu.VMEM((2, depth, 2 * LANES), jnp.bfloat16),

time: 38.8 us -> 38.4 us (0.990)
  Pallas kernels: 37.2 us -> 36.8 us
where the time goes in v7:
time: 38.4 us; the launch traced here: 38.2 us
  Pallas kernels  36.8 us (96%)
  other arithmetic  1.33 us (3%)
    pallas_call x1, Pallas kernels, by_frequency(): pl.pallas_call(functools.partial(kernel, sizes), out_shape=jax.ShapeDtype...  36.8 us
    mul x1, other arithmetic, by_frequency(): return sums * jnp.float32(1.0 / (windows * n_win))  1.33 us

profile of v7, /device:TPU:1, one launch (start us, length us, event | category | flops | bytes accessed | tf_op | source)
XLA Modules:
  0.0 38.2 jit_solution(6205856348143975404)
XLA Ops:
  0.0 36.8 %shard_map.46 = f32[4,1024]{1,0:T(4,128)} custom-call(bf16[7,16,4096]{2,1,0:T(8,128)(2,1)} %bitcast.2, s32[3,7,7]{2,1,0:T(8,128)} %bitcast.3, s32[8]{0:T(128)} %count_ref.1, s32[16]{0:T(128)} %order_ref.1), custom_call_target="tpu_custom_call" | custom-call | flops 38535168 | bytes 917504 | tf_op jit(solution)/shard_map/pallas_call | solution.py:331
  36.8 1.3 %broadcast_multiply_fusion = f32[4,1024]{1,0:T(4,128)} fusion(f32[4,1024]{1,0:T(4,128)} %shard_map.46), kind=kLoop, calls=%fused_computation | loop fusion | flops 4096 | bytes 32768 | tf_op jit(solution)/shard_map/mul | solution.py:368

commit v8 on v7

--- a/solution.py
+++ b/solution.py
@@ -73,14 +73,16 @@
             return lax.rem(me + k, n_sta)
         digits, bit = me, 1
         while bit < n_sta:
-            if k & bit:
-                digits = digits + bit - 2 * bit * lax.rem(digits // bit, 2)
+            of_me, of_k = lax.rem(me // bit, 2), lax.rem(k // bit, 2)
+            digits = digits + bit * of_k * (1 - 2 * of_me)
             bit *= 2
         return digits
 
     far_half = list(range(n_sta // 2, n_sta))
-    near_half = list(range(1, n_sta // 2)) + [None]
-    turns = [k for pair in zip(far_half, near_half) for k in pair if k is not None]
+    near_half = list(range(1, n_sta // 2))
+    even = [k for pair in zip(far_half, near_half) for k in pair] + far_half[-1:]
+    odd = [k for pair in zip(near_half, far_half) for k in pair] + far_half[-1:]
+    turns = [jnp.where(lax.rem(g, 2) == 0, k, l) for k, l in zip(even, odd)]
 
     def share_of(dest, c, part):
         col = pl.multiple_of(part * width + dest * share + c * LANES, LANES)

time: 38.4 us -> 38.5 us (level)
  no operation moved by 1% of the time
where the time goes in v8:
time: 38.5 us; the launch traced here: 38.2 us
  Pallas kernels  36.9 us (96%)
  other arithmetic  1.33 us (3%)
    pallas_call x1, Pallas kernels, by_frequency(): pl.pallas_call(functools.partial(kernel, sizes), out_shape=jax.ShapeDtype...  36.9 us
    mul x1, other arithmetic, by_frequency(): return sums * jnp.float32(1.0 / (windows * n_win))  1.33 us

profile of v8, /device:TPU:1, one launch (start us, length us, event | category | flops | bytes accessed | tf_op | source)
XLA Modules:
  0.0 38.2 jit_solution(13558436774380265175)
XLA Ops:
  0.0 36.9 %shard_map.46 = f32[4,1024]{1,0:T(4,128)} custom-call(bf16[7,16,4096]{2,1,0:T(8,128)(2,1)} %bitcast.2, s32[3,7,7]{2,1,0:T(8,128)} %bitcast.3, s32[8]{0:T(128)} %count_ref.1, s32[16]{0:T(128)} %order_ref.1), custom_call_target="tpu_custom_call" | custom-call | flops 38535168 | bytes 917504 | tf_op jit(solution)/shard_map/pallas_call | solution.py:333
  36.9 1.3 %broadcast_multiply_fusion = f32[4,1024]{1,0:T(4,128)} fusion(f32[4,1024]{1,0:T(4,128)} %shard_map.46), kind=kLoop, calls=%fused_computation | loop fusion | flops 4096 | bytes 32768 | tf_op jit(solution)/shard_map/mul | solution.py:370

commit v9 on v7

--- a/solution.py
+++ b/solution.py
@@ -102,13 +102,6 @@
             device_id_type=MESH,
         )
 
-    for c in range(chunks):
-        for k in turns:
-            for part in range(2):
-                stage_copy(c, k, part).start()
-        for part in range(2):
-            own_copy(c, part).start()
-
     barrier = pltpu.get_barrier_semaphore()
     for t in range(1, n_sta):
         pl.semaphore_signal(
@@ -118,6 +111,25 @@
         pl.semaphore_signal(
             barrier, inc=1, device_id=(me, lax.rem(g + t, n_win)), device_id_type=MESH
         )
+    def stage_chunk(c):
+        for k in turns:
+            for part in range(2):
+                stage_copy(c, k, part).start()
+
+    stage_chunk(0)
+    pl.semaphore_wait(barrier, n_sta + n_win - 2)
+
+    for k in turns:
+        for part in range(2):
+            stage_copy(0, k, part).wait()
+        spectra_copy(0, k).start()
+
+    for c in range(1, chunks):
+        stage_chunk(c)
+    for c in range(chunks):
+        for part in range(2):
+            own_copy(c, part).start()
+
     lane = lax.broadcasted_iota(jnp.int32, (1, lab.shape[2]), 1)
     row = jnp.full((1, lab.shape[2]), -2, jnp.int32)
     for r in range(rounds):
@@ -125,6 +137,25 @@
             for i in range(stations):
                 row = jnp.where(lane == (r * ROWS + j) * ROWS + i, bins_ref[r, i, j], row)
     lab[pl.ds(me, 1)] = row[None]
+
+    def label_copy(k):
+        return pltpu.make_async_remote_copy(
+            src_ref=lab.at[me],
+            dst_ref=lab.at[me],
+            send_sem=lab_send.at[k],
+            recv_sem=lab_recv.at[me],
+            device_id=(lax.rem(me + k, n_sta), g),
+            device_id_type=MESH,
+        )
+
+    for k in range(1, n_sta):
+        label_copy(k).start()
+
+    for c in range(1, chunks):
+        for k in turns:
+            for part in range(2):
+                stage_copy(c, k, part).wait()
+            spectra_copy(c, k).start()
 
     sub = lax.broadcasted_iota(jnp.int32, (n_sta * CAP, LANES), 0)
     slot = jnp.full((n_sta * CAP, LANES), -1, jnp.int32)
@@ -138,32 +169,6 @@
     slots[...] = slot
 
     wide[...] = jnp.zeros_like(wide)
-    pl.semaphore_wait(barrier, n_sta + n_win - 2)
-
-    def label_copy(k):
-        return pltpu.make_async_remote_copy(
-            src_ref=lab.at[me],
-            dst_ref=lab.at[me],
-            send_sem=lab_send.at[k],
-            recv_sem=lab_recv.at[me],
-            device_id=(lax.rem(me + k, n_sta), g),
-            device_id_type=MESH,
-        )
-
-    for k in range(1, n_sta):
-        label_copy(k).start()
-
-    for k in turns:
-        for part in range(2):
-            stage_copy(0, k, part).wait()
-        spectra_copy(0, k).start()
-
-    for c in range(1, chunks):
-        for k in turns:
-            for part in range(2):
-                stage_copy(c, k, part).wait()
-            spectra_copy(c, k).start()
-
     for k in range(1, n_sta):
         src = lax.rem(me - k + n_sta, n_sta)
         pltpu.make_async_remote_copy(

time: 38.4 us -> 39.9 us (1.039)
  Pallas kernels: 36.8 us -> 38.2 us
    pallas_call x1, Pallas kernels: 36.8 us -> 38.2 us  [by_frequency(): pl.pallas_call(functools.partial(kernel, sizes), out_shape=jax.ShapeDtype...]
where the time goes in v9:
time: 39.9 us; the launch traced here: 39.5 us
  Pallas kernels  38.2 us (96%)
  other arithmetic  1.33 us (3%)
    pallas_call x1, Pallas kernels, by_frequency(): pl.pallas_call(functools.partial(kernel, sizes), out_shape=jax.ShapeDtype...  38.2 us
    mul x1, other arithmetic, by_frequency(): return sums * jnp.float32(1.0 / (windows * n_win))  1.33 us

profile of v9, /device:TPU:1, one launch (start us, length us, event | category | flops | bytes accessed | tf_op | source)
XLA Modules:
  0.0 39.5 jit_solution(11654255576354988793)
XLA Ops:
  0.0 38.2 %shard_map.46 = f32[4,1024]{1,0:T(4,128)} custom-call(bf16[7,16,4096]{2,1,0:T(8,128)(2,1)} %bitcast.2, s32[3,7,7]{2,1,0:T(8,128)} %bitcast.3, s32[8]{0:T(128)} %count_ref.1, s32[16]{0:T(128)} %order_ref.1), custom_call_target="tpu_custom_call" | custom-call | flops 38535168 | bytes 917504 | tf_op jit(solution)/shard_map/pallas_call | solution.py:336
  38.2 1.3 %broadcast_multiply_fusion = f32[4,1024]{1,0:T(4,128)} fusion(f32[4,1024]{1,0:T(4,128)} %shard_map.46), kind=kLoop, calls=%fused_computation | loop fusion | flops 4096 | bytes 32768 | tf_op jit(solution)/shard_map/mul | solution.py:373

commit v10 on v7

--- a/solution.py
+++ b/solution.py
@@ -126,6 +126,32 @@
                 row = jnp.where(lane == (r * ROWS + j) * ROWS + i, bins_ref[r, i, j], row)
     lab[pl.ds(me, 1)] = row[None]
 
+    pl.semaphore_wait(barrier, n_sta + n_win - 2)
+
+    def label_copy(k):
+        return pltpu.make_async_remote_copy(
+            src_ref=lab.at[me],
+            dst_ref=lab.at[me],
+            send_sem=lab_send.at[k],
+            recv_sem=lab_recv.at[me],
+            device_id=(lax.rem(me + k, n_sta), g),
+            device_id_type=MESH,
+        )
+
+    for k in range(1, n_sta):
+        label_copy(k).start()
+
+    for k in turns:
+        for part in range(2):
+            stage_copy(0, k, part).wait()
+        spectra_copy(0, k).start()
+
+    for c in range(1, chunks):
+        for k in turns:
+            for part in range(2):
+                stage_copy(c, k, part).wait()
+            spectra_copy(c, k).start()
+
     sub = lax.broadcasted_iota(jnp.int32, (n_sta * CAP, LANES), 0)
     slot = jnp.full((n_sta * CAP, LANES), -1, jnp.int32)
     start = jnp.int32(0)
@@ -138,32 +164,6 @@
     slots[...] = slot
 
     wide[...] = jnp.zeros_like(wide)
-    pl.semaphore_wait(barrier, n_sta + n_win - 2)
-
-    def label_copy(k):
-        return pltpu.make_async_remote_copy(
-            src_ref=lab.at[me],
-            dst_ref=lab.at[me],
-            send_sem=lab_send.at[k],
-            recv_sem=lab_recv.at[me],
-            device_id=(lax.rem(me + k, n_sta), g),
-            device_id_type=MESH,
-        )
-
-    for k in range(1, n_sta):
-        label_copy(k).start()
-
-    for k in turns:
-        for part in range(2):
-            stage_copy(0, k, part).wait()
-        spectra_copy(0, k).start()
-
-    for c in range(1, chunks):
-        for k in turns:
-            for part in range(2):
-                stage_copy(c, k, part).wait()
-            spectra_copy(c, k).start()
-
     for k in range(1, n_sta):
         src = lax.rem(me - k + n_sta, n_sta)
         pltpu.make_async_remote_copy(

time: 38.4 us -> 38.4 us (level)
  no operation moved by 1% of the time
where the time goes in v10:
time: 38.4 us; the launch traced here: 38.2 us
  Pallas kernels  36.8 us (96%)
  other arithmetic  1.33 us (3%)
    pallas_call x1, Pallas kernels, by_frequency(): pl.pallas_call(functools.partial(kernel, sizes), out_shape=jax.ShapeDtype...  36.8 us
    mul x1, other arithmetic, by_frequency(): return sums * jnp.float32(1.0 / (windows * n_win))  1.33 us

profile of v10, /device:TPU:1, one launch (start us, length us, event | category | flops | bytes accessed | tf_op | source)
XLA Modules:
  0.0 38.2 jit_solution(582021208465192279)
XLA Ops:
  0.0 36.8 %shard_map.46 = f32[4,1024]{1,0:T(4,128)} custom-call(bf16[7,16,4096]{2,1,0:T(8,128)(2,1)} %bitcast.2, s32[3,7,7]{2,1,0:T(8,128)} %bitcast.3, s32[8]{0:T(128)} %count_ref.1, s32[16]{0:T(128)} %order_ref.1), custom_call_target="tpu_custom_call" | custom-call | flops 38535168 | bytes 917504 | tf_op jit(solution)/shard_map/pallas_call | solution.py:331
  36.8 1.3 %broadcast_multiply_fusion = f32[4,1024]{1,0:T(4,128)} fusion(f32[4,1024]{1,0:T(4,128)} %shard_map.46), kind=kLoop, calls=%fused_computation | loop fusion | flops 4096 | bytes 32768 | tf_op jit(solution)/shard_map/mul | solution.py:368
